TPU v7x, 32 devices: a whole 2x2x4 slice. The times are simulated.
32 devices in a mesh: ctx: 8 (over z, x), tp: 4 (over y, core).
Axes of the slice: x: 2, y: 2, z: 4, core: 2. Of those that a mesh axis runs over, the one named last changes fastest.
Arguments:
- inputs: bfloat16 [1024, 4096], P('ctx'), may hold values from -6 to 6
- w_query: bfloat16 [4096, 4096], P(None, 'tp'), may hold values from -0.109375 to 0.109375
- w_key: bfloat16 [4096, 512], P(None, 'tp'), may hold values from -0.109375 to 0.109375
- w_value: bfloat16 [4096, 512], P(None, 'tp'), may hold values from -0.09375 to 0.09375
- attn_out: bfloat16 [1024, 4096], P('ctx', 'tp'), may hold values from -6 to 6
- d_out: bfloat16 [1024, 4096], P('ctx', 'tp'), may hold values from -6 to 6
- block_order: int32 [16], replicated, may hold values from 0 to 15, each once
Outputs:
- d_input: bfloat16 [1024, 4096], P('ctx', 'tp')
Inputs may be any that keep to these rules, and one draw needn't show every extreme that they name: `block_order`: a permutation of the sequence blocks.
All inputs are finite; a program needn't handle non-finite values.
Results may differ from a plain program's by a relative error of at most 0.012.
Values may be sent and summed in bfloat16 or wider, within the bound.
A program may use at most 192 MiB of HBM per device.

v0:
```python
import functools
import math

import jax
import jax.numpy as jnp
from jax import lax
from jax.experimental import pallas as pl
from jax.experimental.pallas import tpu as pltpu
from jax.sharding import PartitionSpec as P

MESH = pl.DeviceIdType.MESH
F32 = jnp.float32
BF16 = jnp.bfloat16
big_negative = -1e30
q_chunks = 4
pieces = 4
kept_scores = 8 * 2**20


def dot(a, b):
    return jnp.dot(a, b, preferred_element_type=F32)


def kernel(
    n, m, order, x_hbm, wq_hbm, wk_hbm, wv_hbm, ao_hbm, do_hbm, out,
    x, wq, wkv, ao, do, q_acc, q_rows, q_cols, do_rows, do_cols, delta, top, total,
    kk, vv, scores, p_b, ds_b, dq_cols, part, from_partner, z_out, z_in, dq_b, grads,
    t_out, t_in, y_out, y_in,
    load_sem, side_sem, kv_send, kv_fwd, kv_recv, part_send, part_recv, z_send, z_recv,
    t_send, t_recv, y_send, y_recv,
):
    tokens, width = x.shape
    head_dim = wk_hbm.shape[1]
    heads = wq.shape[1] // head_dim
    rows = heads * tokens
    span = tokens // 2
    scale = head_dim ** (-0.5)
    scale2 = scale * math.log2(math.e)
    nz, na = n // 2, m // 2
    me, mt = lax.axis_index("ctx"), lax.axis_index("tp")
    z, side = me // 2, lax.rem(me, 2)
    other = 1 - side
    partner = z * 2 + other
    pair, core = mt // 2, lax.rem(mt, 2)
    t_partner = pair * 2 + 1 - core
    features = width // m

    def peer(j):
        return lax.rem(z + j, nz)

    def local(src, dst, sem):
        return pltpu.make_async_copy(src, dst, sem)

    def remote(src, dst, send, recv, axis, to):
        return pltpu.make_async_remote_copy(
            src_ref=src, dst_ref=dst, send_sem=send, recv_sem=recv,
            device_id={axis: to}, device_id_type=MESH,
        )

    depth = width // q_chunks

    steps = [slice(i * depth, (i + 1) * depth) for i in range(q_chunks)]
    down = [pl.ds(i * depth, depth) for i in range(q_chunks)]
    x_loads = [
        local(x_hbm.at[:, d], x.at[:, d], load_sem.at[0, i]) for i, d in enumerate(down)
    ]
    wk_loads = [
        local(wk_hbm.at[d], wkv.at[d, pl.ds(0, head_dim)], load_sem.at[1, i])
        for i, d in enumerate(down)
    ]
    wv_loads = [
        local(wv_hbm.at[d], wkv.at[d, pl.ds(head_dim, head_dim)], load_sem.at[2, i])
        for i, d in enumerate(down)
    ]
    wq_loads = [local(wq_hbm.at[d], wq.at[d], load_sem.at[3, i]) for i, d in enumerate(down)]
    side_loads = [local(do_hbm, do, side_sem.at[0]), local(ao_hbm, ao, side_sem.at[1])]
    for i in range(q_chunks):
        x_loads[i].start()
        wk_loads[i].start()
    for copy in wv_loads + side_loads:
        copy.start()

    barrier = pltpu.get_barrier_semaphore()

    def greet(axis, to):
        pl.semaphore_signal(barrier, inc=1, device_id={axis: to}, device_id_type=MESH)

    greet("ctx", partner)
    greet("tp", t_partner)

    def greet_z(j, c):
        greet("ctx", peer(j) * 2 + side)
        return c

    lax.fori_loop(1, nz, greet_z, 0)
    for b in range(1, na):
        greet("tp", lax.rem(pair + b, na) * 2 + core)

    def kv_copy(kind, slot, send, to):
        held = (kk, vv)[kind]
        return remote(held.at[slot], held.at[slot], send, kv_recv.at[kind, slot], "ctx", to)

    def kv_out(kind, j):
        return kv_copy(kind, me, kv_send.at[kind, j], peer(j) * 2 + side)

    def forward(kind, j):
        return kv_copy(kind, peer(j) * 2 + side, kv_fwd.at[kind, j], partner)

    def send_own(kind):
        def start_out(j, c):
            kv_out(kind, j).start()
            return c

        lax.fori_loop(1, nz, start_out, 0)
        forward(kind, 0).start()

    def pass_on(kind, j, c):
        forward(kind, j).wait_recv()
        forward(kind, j).start()
        return c

    pass_key = functools.partial(pass_on, 0)

    keys = None
    for i in range(q_chunks):
        x_loads[i].wait()
        wk_loads[i].wait()
        wq_loads[i].start()
        piece = dot(x[:, steps[i]], wkv[steps[i], :head_dim])
        keys = piece if i == 0 else keys + piece
    kk[me] = keys.astype(BF16)
    pl.semaphore_wait(barrier, nz + na)
    send_own(0)
    for copy in wv_loads:
        copy.wait()
    vv[me] = dot(x[...], wkv[:, head_dim:]).astype(BF16)
    send_own(1)

    for copy in side_loads:
        copy.wait()
    for h in range(heads):
        r, c = slice(h * tokens, (h + 1) * tokens), slice(h * head_dim, (h + 1) * head_dim)
        do_h = do[:, c]
        do_rows[r, :] = do_h
        do_cols[:, r] = do_h.T
        both = do_h.astype(F32) * ao[:, c].astype(F32)
        delta[:, r] = jnp.sum(both.T, axis=0, keepdims=True)

    for i in range(q_chunks):
        wq_loads[i].wait()
        piece = dot(x[:, steps[i]], wq[steps[i], :])
        q_acc[...] = piece if i == 0 else q_acc[...] + piece
        last = nz if i == q_chunks - 2 else min(i + 2, nz)
        if i < q_chunks - 1:
            lax.fori_loop(min(i + 1, nz), last, pass_key, 0)
    for h in range(heads):
        r, c = slice(h * tokens, (h + 1) * tokens), slice(h * head_dim, (h + 1) * head_dim)
        q_h = q_acc[:, c].astype(BF16)
        q_rows[r, :] = q_h
        q_cols[:, r] = q_h.T

    lanes = max(2 * tokens, 256) if heads % 2 == 0 else tokens
    chunks = rows // lanes
    lane = lax.rem(lax.broadcasted_iota(jnp.int32, (1, lanes), 1), tokens)
    o0, o1 = order[me * 2], order[me * 2 + 1]
    query_pos = jnp.where(lane < span, o0 * span + lane, o1 * span + lane - span)
    key_row = lax.broadcasted_iota(jnp.int32, (2 * tokens, 1), 0)

    def allowed(to):
        key_pos = order[to * 4] * span + key_row
        for i in range(1, 4):
            key_pos = jnp.where(
                key_row >= i * span, order[to * 4 + i] * span + key_row - i * span, key_pos
            )
        return key_pos <= query_pos

    def pair_of(held, to):
        return held[pl.ds(to * 2, 2)].reshape(2 * tokens, head_dim)

    keep = scores.shape[0] == nz
    top[...] = jnp.full_like(top, big_negative)
    total[...] = jnp.zeros_like(total)

    def stats(j, carry):
        to = peer(j)
        kv_copy(0, to * 2 + other, kv_fwd.at[0, j], partner).wait_recv()
        mask = allowed(to)
        keys = pair_of(kk, to)
        for c in range(chunks):
            at = slice(c * lanes, (c + 1) * lanes)
            s = jnp.where(mask, dot(keys, q_cols[:, at]) * scale2, big_negative)
            if keep:
                scores[j, :, at] = s
            old = top[:, at]
            new = jnp.maximum(old, jnp.max(s, axis=0, keepdims=True))
            total[:, at] = total[:, at] * jnp.exp2(old - new) + jnp.sum(
                jnp.exp2(s - new), axis=0, keepdims=True
            )
            top[:, at] = new

        @pl.when(j + 1 < nz)
        def _():
            pass_on(1, j + 1, 0)

        return carry

    lax.fori_loop(0, nz, stats, 0)
    top[...] = top[...] + jnp.log(total[...]) * math.log2(math.e)
    dq_cols[...] = jnp.zeros_like(dq_cols)

    def to_partner(j):
        to = peer(j)
        return remote(
            part.at[to, other], from_partner.at[to], part_send.at[j], part_recv.at[j],
            "ctx", partner,
        )

    def to_owner(j):
        to = peer(j)
        return remote(
            z_out.at[j], z_in.at[j], z_send.at[j], z_recv.at[j], "ctx", to * 2 + side
        )

    def settle(j):
        to = peer(j)
        to_partner(j).wait_recv()
        both = part[to, side].astype(F32) + from_partner[to].astype(F32)
        z_out[j] = both.astype(BF16)
        to_owner(j).start()

    def grad(i, carry):
        j = lax.rem(i + 1, nz)
        to = peer(j)
        mask = None if keep else allowed(to)
        kv_copy(1, to * 2 + other, kv_fwd.at[1, j], partner).wait_recv()
        keys, values = pair_of(kk, to), pair_of(vv, to)
        for c in range(chunks):
            at = slice(c * lanes, (c + 1) * lanes)
            if keep:
                s = scores[j, :, at]
            else:
                s = jnp.where(mask, dot(keys, q_cols[:, at]) * scale2, big_negative)
            p = jnp.exp2(s - top[:, at])
            dp = dot(values, do_cols[:, at])
            p_b[:, at] = p.astype(BF16)
            ds_b[:, at] = (p * (dp - delta[:, at])).astype(BF16)
        dk = dot(ds_b[...], q_rows[...]) * scale
        dv = dot(p_b[...], do_rows[...])
        part[to, :, :, :head_dim] = dk.astype(BF16).reshape(2, tokens, head_dim)
        part[to, :, :, head_dim:] = dv.astype(BF16).reshape(2, tokens, head_dim)
        to_partner(j).start()
        dq_cols[...] += dot(keys.T, ds_b[...])

        @pl.when(i > 1)
        def _():
            settle(i - 1)

        return carry

    lax.fori_loop(0, nz, grad, 0)

    for h in range(heads):
        dq_b[h * head_dim:(h + 1) * head_dim, :] = (
            dq_cols[:, h * tokens:(h + 1) * tokens] * scale
        ).astype(BF16)
    tile = min(512, width)

    def query_terms(i, carry):
        at = pl.ds(pl.multiple_of(i * tile, tile), tile)
        grads[at, :] = dot(wq[at, :], dq_b[...])
        return carry

    early = max(1, width // tile // 4)
    lax.fori_loop(0, early, query_terms, 0)
    if nz > 1:
        settle(nz - 1)
    lax.fori_loop(early, width // tile, query_terms, 0)

    to_partner(0).wait_recv()
    mine = part[z, side].astype(F32) + from_partner[z].astype(F32)

    def gather_terms(j, acc):
        to_owner(j).wait_recv()
        return acc + z_in[j].astype(F32)

    mine = lax.fori_loop(1, nz, gather_terms, mine)
    dkv = mine.T.astype(BF16)

    size = features // pieces

    def rows_of(b, c, i):
        start = (lax.rem(pair + b, na) * 2 + c) * features + i * size
        return pl.ds(pl.multiple_of(start, size), size)

    def to_core(b, i):
        return remote(
            t_out.at[b, i], t_in.at[b, i], t_send.at[b, i], t_recv.at[b, i], "tp", t_partner
        )

    def across(b, i):
        to = lax.rem(pair + b, na) * 2 + core
        return remote(y_out.at[b, i], y_in.at[b, i], y_send.at[b, i], y_recv.at[b, i], "tp", to)

    for b in [b % na for b in range(1, na + 1)]:
        for i in range(pieces):
            at = rows_of(b, 1 - core, i)
            t_out[b, i] = (grads[at, :] + dot(wkv[at, :], dkv)).astype(BF16)
            to_core(b, i).start()
        for i in range(pieces):
            at = rows_of(b, core, i)
            term = grads[at, :] + dot(wkv[at, :], dkv)
            to_core(b, i).wait_recv()
            term = term + t_in[b, i].astype(F32)
            if b > 0:
                y_out[b, i] = term.astype(BF16)
                across(b, i).start()
            else:
                grads[at, :] = term
    for i in range(pieces):
        term = grads[rows_of(0, core, i), :]
        for b in range(1, na):
            across(b, i).wait_recv()
            term = term + y_in[b, i].astype(F32)
        out[:, i * size:(i + 1) * size] = term.T.astype(BF16)

    def drain(j, carry):
        forward(0, j).wait_send()
        forward(1, j).wait_send()
        to_partner(j).wait_send()
        return carry

    def drain_z(j, carry):
        kv_out(0, j).wait_send()
        kv_out(1, j).wait_send()
        to_owner(j).wait_send()
        return carry

    lax.fori_loop(0, nz, drain, 0)
    lax.fori_loop(1, nz, drain_z, 0)
    for b in range(na):
        for i in range(pieces):
            to_core(b, i).wait_send()
            if b > 0:
                across(b, i).wait_send()


def on_device(n, m, inputs, w_query, w_key, w_value, attn_out, d_out, block_order):
    tokens, width = inputs.shape
    head_dim = w_key.shape[1]
    local_width = w_query.shape[1]
    rows = local_width // head_dim * tokens
    features = width // m
    nz, na = n // 2, m // 2
    keep = n * tokens * rows * 4 <= kept_scores
    vmem, dma = pltpu.VMEM, pltpu.SemaphoreType.DMA
    block = (tokens, 2 * head_dim)
    scratch = [
        vmem((tokens, width), BF16),
        vmem((width, local_width), BF16),
        vmem((width, 2 * head_dim), BF16),
        vmem((tokens, local_width), BF16),
        vmem((tokens, local_width), BF16),
        vmem((tokens, local_width), F32),
        vmem((rows, head_dim), BF16),
        vmem((head_dim, rows), BF16),
        vmem((rows, head_dim), BF16),
        vmem((head_dim, rows), BF16),
        vmem((1, rows), F32),
        vmem((1, rows), F32),
        vmem((1, rows), F32),
        vmem((n, tokens, head_dim), BF16),
        vmem((n, tokens, head_dim), BF16),
        vmem((nz if keep else 1, 2 * tokens, rows), F32),
        vmem((2 * tokens, rows), BF16),
        vmem((2 * tokens, rows), BF16),
        vmem((head_dim, rows), F32),
        vmem((nz, 2, *block), BF16),
        vmem((nz, *block), BF16),
        vmem((nz, *block), BF16),
        vmem((nz, *block), BF16),
        vmem((local_width, tokens), BF16),
        vmem((width, tokens), F32),
        vmem((na, pieces, features // pieces, tokens), BF16),
        vmem((na, pieces, features // pieces, tokens), BF16),
        vmem((na, pieces, features // pieces, tokens), BF16),
        vmem((na, pieces, features // pieces, tokens), BF16),
        dma((4, q_chunks)), dma((2,)), dma((2, nz)), dma((2, nz)), dma((2, n)),
        dma((nz,)), dma((nz,)), dma((nz,)), dma((nz,)),
        dma((na, pieces)), dma((na, pieces)), dma((na, pieces)), dma((na, pieces)),
    ]
    seq = tokens * n
    flops = 2 * tokens * (2 * width * (local_width + 2 * head_dim) + 6 * seq * local_width)
    return pl.pallas_call(
        functools.partial(kernel, n, m),
        out_shape=pltpu.VMEM((tokens, features), BF16),
        in_specs=[pl.BlockSpec(memory_space=pltpu.SMEM)] + [pl.BlockSpec(memory_space=pl.ANY)] * 6,
        out_specs=pl.BlockSpec(memory_space=pltpu.VMEM),
        scratch_shapes=scratch,
        compiler_params=pltpu.CompilerParams(
            collective_id=0, has_side_effects=True, vmem_limit_bytes=58 * 2**20
        ),
        cost_estimate=pl.CostEstimate(
            flops=flops, bytes_accessed=2 * width * (local_width + 2 * head_dim + 2 * tokens),
            transcendentals=2 * rows * seq,
        ),
    )(block_order, inputs, w_query, w_key, w_value, attn_out, d_out)


def solution(mesh):
    placed = (
        P("ctx", None),
        P(None, "tp"),
        P(None, "tp"),
        P(None, "tp"),
        P("ctx", "tp"),
        P("ctx", "tp"),
        P(),
    )
    return jax.shard_map(
        functools.partial(on_device, mesh.shape["ctx"], mesh.shape["tp"]),
        mesh=mesh, in_specs=placed, out_specs=P("ctx", "tp"), check_vma=False,
    )
```

profile of v0, /device:TPU:0, one launch (start us, length us, event | category | flops | bytes accessed | tf_op | source)
XLA Modules:
  0.0 38.2 jit_solution(9754446575487848293)
XLA Ops:
  0.0 37.5 %shard_map.73 = bf16[128,1024]{1,0:T(8,128)(2,1)S(1)} custom-call(s32[16]{0:T(128)} %order.1, bf16[128,4096]{1,0:T(8,128)(2,1)} %x_hbm.1, bf16[4096,1024]{1,0:T(8,128)(2,1)} %wq_hbm.1, bf16[4096,128]{1,0:T(8,128)(2,1)} %wk_hbm.1, bf16[4096,128]{1,0:T(8,128)(2,1)} %wv_hbm.1, bf16[128,1024]{1,0:T(8,128)(2,1)} %ao_hbm.1, bf16[128,1024]{1,0:T(8,128)(2,1)} %do_hbm.1), custom_call_target="tpu_custom_call" | custom-call | flops 4294967296 | bytes 12582912 | tf_op jit(solution)/shard_map/pallas_call | solution.py:393
  37.5 0.7 %copy.9 = bf16[128,1024]{1,0:T(8,128)(2,1)} copy(bf16[128,1024]{1,0:T(8,128)(2,1)S(1)} %shard_map.73) | data formatting | bytes 524288
where the time goes:
time: 38.4 us; the launch traced here: 38.2 us
  Pallas kernels  37.5 us (98%)
  local copies, waits for them, and re-layouts  0.71 us (2%)
    pallas_call x1, Pallas kernels, on_device(): pl.pallas_call(functools.partial(kernel, n, m), out_shape=pltpu.VMEM((tok...  37.5 us

commit v1 on v0

--- a/solution.py
+++ b/solution.py
@@ -13,7 +13,7 @@
 BF16 = jnp.bfloat16
 big_negative = -1e30
 q_chunks = 4
-pieces = 4
+pieces = 2
 kept_scores = 8 * 2**20
 
 
@@ -25,7 +25,7 @@
     n, m, order, x_hbm, wq_hbm, wk_hbm, wv_hbm, ao_hbm, do_hbm, out,
     x, wq, wkv, ao, do, q_acc, q_rows, q_cols, do_rows, do_cols, delta, top, total,
     kk, vv, scores, p_b, ds_b, dq_cols, part, from_partner, z_out, z_in, dq_b, grads,
-    t_out, t_in, y_out, y_in,
+    t_out, t_in, y_out, y_in, own,
     load_sem, side_sem, kv_send, kv_fwd, kv_recv, part_send, part_recv, z_send, z_recv,
     t_send, t_recv, y_send, y_recv,
 ):
@@ -208,36 +208,68 @@
     top[...] = top[...] + jnp.log(total[...]) * math.log2(math.e)
     dq_cols[...] = jnp.zeros_like(dq_cols)
 
-    def to_partner(j):
-        to = peer(j)
+    groups = nz // 2
+
+    def pairs_of(g):
+        return 2 * g + 1, lax.rem(2 * g + 2, nz)
+
+    def to_partner(t):
         return remote(
-            part.at[to, other], from_partner.at[to], part_send.at[j], part_recv.at[j],
+            part.at[t, other], from_partner.at[t], part_send.at[t], part_recv.at[t],
             "ctx", partner,
         )
 
-    def to_owner(j):
-        to = peer(j)
+    def to_owner(u, j):
+        t, a = u * groups + (j - 1) // 2, lax.rem(j - 1, 2)
         return remote(
-            z_out.at[j], z_in.at[j], z_send.at[j], z_recv.at[j], "ctx", to * 2 + side
+            z_out.at[t, a], z_in.at[u, j], z_send.at[u, j], z_recv.at[u, j],
+            "ctx", peer(j) * 2 + side,
         )
 
-    def settle(j):
-        to = peer(j)
-        to_partner(j).wait_recv()
-        both = part[to, side].astype(F32) + from_partner[to].astype(F32)
-        z_out[j] = both.astype(BF16)
-        to_owner(j).start()
-
-    def grad(i, carry):
-        j = lax.rem(i + 1, nz)
-        to = peer(j)
-        mask = None if keep else allowed(to)
-        kv_copy(1, to * 2 + other, kv_fwd.at[1, j], partner).wait_recv()
-        keys, values = pair_of(kk, to), pair_of(vv, to)
+    def settle(t):
+        u = t // groups
+        j, j_next = pairs_of(lax.rem(t, groups))
+        to_partner(t).wait_recv()
+        both = part[t, side].astype(F32) + from_partner[t].astype(F32)
+        z_out[t] = both.astype(BF16)
+        to_owner(u, j).start()
+
+        @pl.when(j_next != 0)
+        def _():
+            to_owner(u, j_next).start()
+
+    half_lane = lax.rem(lax.broadcasted_iota(jnp.int32, (2 * tokens, 1), 0), span)
+
+    def grad(t, carry):
+        u, g = t // groups, lax.rem(t, groups)
+        js = pairs_of(g)
+        at_u = pl.ds(pl.multiple_of(u * span, span), span)
+
+        @pl.when(u == 0)
+        def _():
+            for j in js:
+                kv_copy(1, peer(j) * 2 + other, kv_fwd.at[1, j], partner).wait_recv()
+
+        blocks = [(j, d) for d in range(2) for j in js]
+
+        def rows_from(held):
+            return jnp.concatenate([held[peer(j) * 2 + d, at_u] for j, d in blocks], axis=0)
+
+        keys, values = rows_from(kk), rows_from(vv)
+        if not keep:
+            row = lax.broadcasted_iota(jnp.int32, (2 * tokens, 1), 0)
+            key_pos = None
+            for i, (j, d) in enumerate(blocks):
+                pos = order[(peer(j) * 2 + d) * 2 + u] * span + half_lane
+                key_pos = pos if i == 0 else jnp.where(row >= i * span, pos, key_pos)
+            mask = key_pos <= query_pos
         for c in range(chunks):
             at = slice(c * lanes, (c + 1) * lanes)
             if keep:
-                s = scores[j, :, at]
+                s = jnp.concatenate([
+                    scores[j, pl.ds(pl.multiple_of(d * tokens + u * span, span), span), at]
+                    for j, d in blocks
+                ], axis=0)
             else:
                 s = jnp.where(mask, dot(keys, q_cols[:, at]) * scale2, big_negative)
             p = jnp.exp2(s - top[:, at])
@@ -246,14 +278,14 @@
             ds_b[:, at] = (p * (dp - delta[:, at])).astype(BF16)
         dk = dot(ds_b[...], q_rows[...]) * scale
         dv = dot(p_b[...], do_rows[...])
-        part[to, :, :, :head_dim] = dk.astype(BF16).reshape(2, tokens, head_dim)
-        part[to, :, :, head_dim:] = dv.astype(BF16).reshape(2, tokens, head_dim)
-        to_partner(j).start()
+        part[t, :, :, :, :head_dim] = dk.astype(BF16).reshape(2, 2, span, head_dim)
+        part[t, :, :, :, head_dim:] = dv.astype(BF16).reshape(2, 2, span, head_dim)
+        to_partner(t).start()
         dq_cols[...] += dot(keys.T, ds_b[...])
 
-        @pl.when(i > 1)
+        @pl.when(t > 1)
         def _():
-            settle(i - 1)
+            settle(t - 2)
 
         return carry
 
@@ -263,65 +295,83 @@
         dq_b[h * head_dim:(h + 1) * head_dim, :] = (
             dq_cols[:, h * tokens:(h + 1) * tokens] * scale
         ).astype(BF16)
-    tile = min(512, width)
+    low = lax.broadcasted_iota(jnp.int32, (1, 1, tokens), 2) < span
+    tile = 4 * tokens
 
     def query_terms(i, carry):
         at = pl.ds(pl.multiple_of(i * tile, tile), tile)
-        grads[at, :] = dot(wq[at, :], dq_b[...])
+        to = pl.ds(pl.multiple_of(i * (tile // 2), tile // 2), tile // 2)
+        terms = dot(wq[at, :], dq_b[...])
+        turned = pltpu.roll(terms, span, 1).reshape(2, 2, tokens, tokens)
+        terms = terms.reshape(2, 2, tokens, tokens)
+        grads[0, to, :] = jnp.where(low, terms[:, 0], turned[:, 1]).reshape(tile // 2, tokens)
+        grads[1, to, :] = jnp.where(low, turned[:, 0], terms[:, 1]).reshape(tile // 2, tokens)
         return carry
 
-    early = max(1, width // tile // 4)
+    tiles = width // tile
+    early = max(1, tiles * 5 // 8)
     lax.fori_loop(0, early, query_terms, 0)
-    if nz > 1:
-        settle(nz - 1)
-    lax.fori_loop(early, width // tile, query_terms, 0)
-
-    to_partner(0).wait_recv()
-    mine = part[z, side].astype(F32) + from_partner[z].astype(F32)
-
-    def gather_terms(j, acc):
-        to_owner(j).wait_recv()
-        return acc + z_in[j].astype(F32)
-
-    mine = lax.fori_loop(1, nz, gather_terms, mine)
-    dkv = mine.T.astype(BF16)
-
-    size = features // pieces
+    settle(nz - 2)
+    lax.fori_loop(early, tiles, query_terms, 0)
+    settle(nz - 1)
+
+    size = features // 2 // pieces
 
     def rows_of(b, c, i):
-        start = (lax.rem(pair + b, na) * 2 + c) * features + i * size
-        return pl.ds(pl.multiple_of(start, size), size)
-
-    def to_core(b, i):
+        return (lax.rem(pair + b, na) * 2 + c) * (features // 2) + i * size
+
+    def to_core(u, b, i):
         return remote(
-            t_out.at[b, i], t_in.at[b, i], t_send.at[b, i], t_recv.at[b, i], "tp", t_partner
+            t_out.at[u, b, i], t_in.at[u, b, i], t_send.at[u, b, i], t_recv.at[u, b, i],
+            "tp", t_partner,
         )
 
-    def across(b, i):
+    def across(u, b, i):
         to = lax.rem(pair + b, na) * 2 + core
-        return remote(y_out.at[b, i], y_in.at[b, i], y_send.at[b, i], y_recv.at[b, i], "tp", to)
-
-    for b in [b % na for b in range(1, na + 1)]:
+        return remote(
+            y_out.at[u, b, i], y_in.at[u, b, i], y_send.at[u, b, i], y_recv.at[u, b, i], "tp", to
+        )
+
+    for u in range(2):
+        def gather_terms(j, acc):
+            to_owner(u, j).wait_recv()
+            return acc + z_in[u, j].astype(F32)
+
+        mine = z_out[u * groups + groups - 1, 1].astype(F32)
+        mine = lax.fori_loop(1, nz, gather_terms, mine)
+        dkv = jnp.concatenate([mine, mine], axis=0).T.astype(BF16)
+
+        def term_of(b, c, i):
+            start = rows_of(b, c, i)
+            wide = pl.ds(pl.multiple_of(start * 2, size * 2), size * 2)
+            terms = dot(wkv[wide, :], dkv).reshape(size // tokens, 2, tokens, tokens)
+            terms = jnp.where(low, terms[:, 0], terms[:, 1]).reshape(size, tokens)
+            return grads[u, pl.ds(pl.multiple_of(start, size), size), :] + terms
+
+        for b in [b % na for b in range(1, na + 1)]:
+            for i in range(pieces):
+                t_out[u, b, i] = term_of(b, 1 - core, i).astype(BF16)
+                to_core(u, b, i).start()
+            for i in range(pieces):
+                term = term_of(b, core, i)
+                to_core(u, b, i).wait_recv()
+                term = term + t_in[u, b, i].astype(F32)
+                if b > 0:
+                    y_out[u, b, i] = term.astype(BF16)
+                    across(u, b, i).start()
+                else:
+                    own[u, i] = term
+    for u in range(2):
         for i in range(pieces):
-            at = rows_of(b, 1 - core, i)
-            t_out[b, i] = (grads[at, :] + dot(wkv[at, :], dkv)).astype(BF16)
-            to_core(b, i).start()
-        for i in range(pieces):
-            at = rows_of(b, core, i)
-            term = grads[at, :] + dot(wkv[at, :], dkv)
-            to_core(b, i).wait_recv()
-            term = term + t_in[b, i].astype(F32)
-            if b > 0:
-                y_out[b, i] = term.astype(BF16)
-                across(b, i).start()
-            else:
-                grads[at, :] = term
-    for i in range(pieces):
-        term = grads[rows_of(0, core, i), :]
-        for b in range(1, na):
-            across(b, i).wait_recv()
-            term = term + y_in[b, i].astype(F32)
-        out[:, i * size:(i + 1) * size] = term.T.astype(BF16)
+            term = own[u, i]
+            for b in range(1, na):
+                across(u, b, i).wait_recv()
+                term = term + y_in[u, b, i].astype(F32)
+            for k in range(size // tokens):
+                block = term[k * tokens:(k + 1) * tokens].T.astype(BF16)
+                for d in range(2):
+                    at = (i * size + k * tokens) * 2 + d * tokens
+                    out[u * span:(u + 1) * span, at:at + tokens] = block[d * span:(d + 1) * span]
 
     def drain(j, carry):
         forward(0, j).wait_send()
@@ -332,16 +382,18 @@
     def drain_z(j, carry):
         kv_out(0, j).wait_send()
         kv_out(1, j).wait_send()
-        to_owner(j).wait_send()
+        to_owner(0, j).wait_send()
+        to_owner(1, j).wait_send()
         return carry
 
     lax.fori_loop(0, nz, drain, 0)
     lax.fori_loop(1, nz, drain_z, 0)
-    for b in range(na):
-        for i in range(pieces):
-            to_core(b, i).wait_send()
-            if b > 0:
-                across(b, i).wait_send()
+    for u in range(2):
+        for b in range(na):
+            for i in range(pieces):
+                to_core(u, b, i).wait_send()
+                if b > 0:
+                    across(u, b, i).wait_send()
 
 
 def on_device(n, m, inputs, w_query, w_key, w_value, attn_out, d_out, block_order):
@@ -353,7 +405,8 @@
     nz, na = n // 2, m // 2
     keep = n * tokens * rows * 4 <= kept_scores
     vmem, dma = pltpu.VMEM, pltpu.SemaphoreType.DMA
-    block = (tokens, 2 * head_dim)
+    half = (tokens // 2, 2 * head_dim)
+    piece = (pieces, features // 2 // pieces, tokens)
     scratch = [
         vmem((tokens, width), BF16),
         vmem((width, local_width), BF16),
@@ -374,19 +427,20 @@
         vmem((2 * tokens, rows), BF16),
         vmem((2 * tokens, rows), BF16),
         vmem((head_dim, rows), F32),
-        vmem((nz, 2, *block), BF16),
-        vmem((nz, *block), BF16),
-        vmem((nz, *block), BF16),
-        vmem((nz, *block), BF16),
+        vmem((nz, 2, 2, *half), BF16),
+        vmem((nz, 2, *half), BF16),
+        vmem((nz, 2, *half), BF16),
+        vmem((2, nz, *half), BF16),
         vmem((local_width, tokens), BF16),
-        vmem((width, tokens), F32),
-        vmem((na, pieces, features // pieces, tokens), BF16),
-        vmem((na, pieces, features // pieces, tokens), BF16),
-        vmem((na, pieces, features // pieces, tokens), BF16),
-        vmem((na, pieces, features // pieces, tokens), BF16),
+        vmem((2, width // 2, tokens), F32),
+        vmem((2, na, *piece), BF16),
+        vmem((2, na, *piece), BF16),
+        vmem((2, na, *piece), BF16),
+        vmem((2, na, *piece), BF16),
+        vmem((2, *piece), F32),
         dma((4, q_chunks)), dma((2,)), dma((2, nz)), dma((2, nz)), dma((2, n)),
-        dma((nz,)), dma((nz,)), dma((nz,)), dma((nz,)),
-        dma((na, pieces)), dma((na, pieces)), dma((na, pieces)), dma((na, pieces)),
+        dma((nz,)), dma((nz,)), dma((2, nz)), dma((2, nz)),
+        *[dma((2, na, pieces)) for _ in range(4)],
     ]
     seq = tokens * n
     flops = 2 * tokens * (2 * width * (local_width + 2 * head_dim) + 6 * seq * local_width)

time: 38.4 us -> 39.3 us (1.023)
  Pallas kernels: 37.5 us -> 38.4 us
    pallas_call x1, Pallas kernels: 37.5 us -> 38.4 us  [on_device(): pl.pallas_call(functools.partial(kernel, n, m), out_shape=pltpu.VMEM((tok...]
where the time goes in v1:
time: 39.3 us; the launch traced here: 39.2 us
  Pallas kernels  38.4 us (98%)
  local copies, waits for them, and re-layouts  0.71 us (2%)
    pallas_call x1, Pallas kernels, on_device(): pl.pallas_call(functools.partial(kernel, n, m), out_shape=pltpu.VMEM((tok...  38.4 us

profile of v1, /device:TPU:0, one launch (start us, length us, event | category | flops | bytes accessed | tf_op | source)
XLA Modules:
  0.0 39.2 jit_solution(1728590071309418638)
XLA Ops:
  0.0 38.4 %shard_map.73 = bf16[128,1024]{1,0:T(8,128)(2,1)S(1)} custom-call(s32[16]{0:T(128)} %order.1, bf16[128,4096]{1,0:T(8,128)(2,1)} %x_hbm.1, bf16[4096,1024]{1,0:T(8,128)(2,1)} %wq_hbm.1, bf16[4096,128]{1,0:T(8,128)(2,1)} %wk_hbm.1, bf16[4096,128]{1,0:T(8,128)(2,1)} %wv_hbm.1, bf16[128,1024]{1,0:T(8,128)(2,1)} %ao_hbm.1, bf16[128,1024]{1,0:T(8,128)(2,1)} %do_hbm.1), custom_call_target="tpu_custom_call" | custom-call | flops 4294967296 | bytes 12582912 | tf_op jit(solution)/shard_map/pallas_call | solution.py:447
  38.5 0.7 %copy.9 = bf16[128,1024]{1,0:T(8,128)(2,1)} copy(bf16[128,1024]{1,0:T(8,128)(2,1)S(1)} %shard_map.73) | data formatting | bytes 524288
